TPU v7x, 256 devices: a whole 4x4x8 slice. The times are simulated.
256 devices in a mesh: dp: 16 (over y, x), ctx: 16 (over z, core).
Axes of the slice: x: 4, y: 4, z: 8, core: 2. Of those that a mesh axis runs over, the one named last changes fastest.
Arguments:
- frames: bfloat16 [8192, 6144], P('ctx'), may hold values from -6 to 6
- proj_weight: bfloat16 [3, 6144, 4096], P(None, 'ctx', 'dp'), may hold values from -0.078125 to 0.078125
- out_weight: bfloat16 [6144, 4096], P('dp', 'ctx'), may hold values from -0.09375 to 0.09375
- query_gain: float32 [4096], P('dp'), may hold values from 0.5 to 2
- key_gain: float32 [4096], P('dp'), may hold values from 0.5 to 2
- key_tiles: int32 [32, 128, 18], P('dp', 'ctx'), may hold values from 0 to 127, as said below
- key_counts: int32 [32, 128], P('dp', 'ctx'), may hold values from 1 to 18
Outputs:
- mixed: bfloat16 [8192, 6144], P('ctx', 'dp')
Inputs may be any that keep to these rules, and one draw needn't show every extreme that they name: `key_tiles`: tiles have coordinates (frame layer, height, width) on a grid of 16 x 2 x 4, tile number (layer * 2 + height) * 4 + width. For each head and query tile, the first key_counts entries are distinct tiles that differ from the query tile by at most one in each coordinate, the query tile itself among them; the other entries repeat the query tile. In every head some tile lists its whole window.
All inputs are finite; a program needn't handle non-finite values.
Results may differ from a plain program's by a relative error of at most 0.0088.
Values may be sent and summed in bfloat16 or wider, within the bound.
A program may use at most 64 MiB of HBM per device.

v0:
```python
import jax
import jax.numpy as jnp
from jax import lax
from jax.sharding import PartitionSpec as P

TILE = 64
eps = 1e-06


def padded(block, sides, width):
    for axis, dim in sides:
        count = lax.axis_size(axis)
        forward = [(i, i + 1) for i in range(count - 1)]
        backward = [(target, source) for source, target in forward]
        low = lax.ppermute(
            lax.slice_in_dim(block, block.shape[dim] - width, None, axis=dim), axis, forward
        )
        high = lax.ppermute(lax.slice_in_dim(block, 0, width, axis=dim), axis, backward)
        block = jnp.concatenate([low, block, high], axis=dim)
    return block


def normed(rows, gain):
    stat = jnp.mean(rows * rows, axis=-1, keepdims=True)
    return rows * lax.rsqrt(stat + eps) * gain


def attend(query_rows, key_rows, value_rows, tile_ids, tile_counts, first_tile):
    heads = tile_ids.shape[0]
    slots = tile_ids.shape[2]
    head_dim = query_rows.shape[1] // heads
    query_tiles = query_rows.reshape(-1, TILE, heads, head_dim).transpose(2, 0, 1, 3)
    key_tiles = key_rows.reshape(-1, TILE, heads, head_dim).transpose(2, 0, 1, 3)
    value_tiles = value_rows.reshape(-1, TILE, heads, head_dim).transpose(2, 0, 1, 3)
    local_ids = tile_ids - first_tile
    picked_keys = jax.vmap(lambda lookup, indices: lookup[indices])(key_tiles, local_ids)
    picked_values = jax.vmap(lambda lookup, indices: lookup[indices])(value_tiles, local_ids)
    count_q = query_tiles.shape[1]
    picked_keys = picked_keys.reshape(heads, count_q, slots * TILE, head_dim)
    picked_values = picked_values.reshape(heads, count_q, slots * TILE, head_dim)
    scores = jnp.einsum(
        "hqtd,hqsd->hqts", query_tiles, picked_keys, preferred_element_type=jnp.float32
    ) * head_dim ** (-0.5)
    live = (jnp.arange(slots, dtype=jnp.int32)[None, None, :] < tile_counts[:, :, None]).astype(
        jnp.float32
    )
    live = jnp.repeat(live, TILE, axis=2)[:, :, None, :]
    weights = jnp.exp(scores) * live
    totals = jnp.sum(weights, axis=-1, keepdims=True)
    summed = (
        jnp.einsum(
            "hqts,hqsd->hqtd",
            weights.astype(jnp.bfloat16),
            picked_values,
            preferred_element_type=jnp.float32,
        )
        / totals
    )
    return summed.astype(jnp.bfloat16).transpose(1, 2, 0, 3).reshape(-1, heads * head_dim)


def body(frames, proj_weight, out_weight, query_gain, key_gain, key_tiles, key_counts):
    heads = key_tiles.shape[0]
    width = proj_weight.shape[2]
    head_dim = width // heads
    layer_tiles = key_tiles.shape[1]
    tok_count = frames.shape[0]
    columns = frames
    proj = jnp.einsum(
        "tn,cnw->ctw",
        columns,
        lax.all_gather(proj_weight, "ctx", axis=1, tiled=True),
        preferred_element_type=jnp.float32,
    )
    query_rows = normed(proj[0].reshape(-1, heads, head_dim), query_gain.reshape(heads, head_dim))
    key_rows = normed(proj[1].reshape(-1, heads, head_dim), key_gain.reshape(heads, head_dim))
    query_rows = query_rows.reshape(-1, width).astype(jnp.bfloat16)
    key_rows = key_rows.reshape(-1, width).astype(jnp.bfloat16)
    value_rows = proj[2].astype(jnp.bfloat16)
    paired = jnp.stack([key_rows, value_rows], axis=0)
    widened = padded(paired, (("ctx", 1),), tok_count)
    first_tile = (lax.axis_index("ctx") - 1) * layer_tiles
    attended = attend(query_rows, widened[0], widened[1], key_tiles, key_counts, first_tile)
    out_columns = lax.all_gather(out_weight, "ctx", axis=1, tiled=True)
    columns = out_columns
    mixed = lax.dot_general(
        lax.all_gather(attended, "dp", axis=1, tiled=True),
        columns,
        (((1,), (1,)), ((), ())),
        preferred_element_type=jnp.float32,
    )
    return mixed.astype(jnp.bfloat16)


def solution(mesh):
    placed = (
        P("ctx", None),
        P(None, "ctx", "dp"),
        P("dp", "ctx"),
        P("dp"),
        P("dp"),
        P("dp", "ctx", None),
        P("dp", "ctx"),
    )
    return jax.shard_map(
        body, mesh=mesh, in_specs=placed, out_specs=P("ctx", "dp"), check_vma=False
    )
```

profile of v0, /device:TPU:1, one launch (start us, length us, event | category | flops | bytes accessed | tf_op | source)
XLA Modules:
  0.0 201.2 jit_solution(7556137137856312792)
XLA Ops:
  6.5 0.0 all-gather.4.cloned.1.call-start
  6.5 2.1 %copy.12 = bf16[3,384,256]{1,2,0:T(8,128)(2,1)} copy(bf16[3,384,256]{2,1,0:T(8,128)(2,1)} %param.8) | data formatting | bytes 1179648 | tf_op args[1]
  8.7 0.0 all-gather.4.cloned.1.call-update
  8.7 0.0 all-gather.8.cloned.1.call-start
  8.8 0.7 all-gather.8.cloned.1.call-update
  9.5 0.0 all-gather.6.cloned.1.call-start
  9.5 0.7 fusion.23
  10.2 0.0 copy-start.1
  10.2 64.0 %all-gather.4.cloned.1.call-done = bf16[3,6144,256]{1,2,0:T(8,128)(2,1)} async-done(((bf16[3,384,256]{1,2,0:T(8,128)(2,1)}), bf16[3,6144,256]{1,2,0:T(8,128)(2,1)}) %all-gather.4.cloned.1.call-update) | async-done | bytes 9437200 | tf_op jit(solution)/shard_map/all_gather | solution.py:72
  74.2 9.5 %fusion.4 = f32[3,512,256]{1,2,0:T(8,128)S(1)} fusion(bf16[3,6144,256]{1,2,0:T(8,128)(2,1)} %all-gather.4.cloned.1.call-done, bf16[512,6144]{1,0:T(8,128)(2,1)} %param.7), kind=kOutput, calls=%fused_computation.9 | convolution fusion | flops 4831838208 | bytes 17301504 | tf_op jit(solution)/shard_map/tn,cnw->ctw/dot_general | solution.py:69
  83.7 0.0 copy-start.3
  83.8 0.0 copy-start.2
  83.8 0.1 reduce_sum.28
  83.9 0.0 copy-done.1
  83.9 0.2 slice_multiply_fusion.1
  84.1 0.1 pad_maximum_fusion.1
  84.2 1.9 collective-permute-start
  86.1 3.4 %collective-permute-start.1 = (bf16[2,512,256]{1,2,0:T(8,128)(2,1)S(1)}, bf16[2,512,256]{1,2,0:T(8,128)(2,1)}, u32[]{:S(2)}, u32[]{:S(2)}) collective-permute-start(bf16[2,512,256]{1,2,0:T(8,128)(2,1)S(1)} %pad_maximum_fusion.1), channel_id=1, source_target_pairs={{1,0},{2,1},{3,2},{4,3},{5,4},{6,5},{7,6},{8,7},{9,8},{10,9},{11,1... | collective-permute-start | bytes 1572872 | tf_op jit(solution)/shard_map/ppermute | solution.py:18
  89.5 0.0 copy-done.3
  89.5 0.1 fusion.24
  89.5 0.1 reshape.68
  89.6 0.1 broadcast_in_dim.5
  89.7 0.1 mul.100
  89.8 0.2 copy.13
  90.0 0.3 reshape_squeeze.10
  90.3 0.1 reduce_sum.27
  90.4 0.1 copy.14
  90.6 0.0 copy-done.2
  90.6 0.7 fusion.18
  91.3 3.3 %collective-permute-done = bf16[2,512,256]{1,2,0:T(8,128)(2,1)} collective-permute-done((bf16[2,512,256]{1,2,0:T(8,128)(2,1)S(1)}, bf16[2,512,256]{1,2,0:T(8,128)(2,1)}, u32[]{:S(2)}, u32[]{:S(2)}) %collective-permute-start) | collective-permute-done | bytes 524320 | tf_op jit(solution)/shard_map/ppermute | solution.py:15
  94.6 4.4 %collective-permute-done.1 = bf16[2,512,256]{1,2,0:T(8,128)(2,1)} collective-permute-done((bf16[2,512,256]{1,2,0:T(8,128)(2,1)S(1)}, bf16[2,512,256]{1,2,0:T(8,128)(2,1)}, u32[]{:S(2)}, u32[]{:S(2)}) %collective-permute-start.1) | collective-permute-done | bytes 524320 | tf_op jit(solution)/shard_map/ppermute | solution.py:18
  99.0 1.3 pad_maximum_fusion
  100.3 1.0 fusion.25
  101.3 0.9 reshape.88
  102.2 1.0 copy.16
  103.2 2.4 %reshape.89 = bf16[24,64,2,128]{1,0,3,2:T(8,128)(2,1)S(1)} reshape(bf16[1,1536,256]{1,2,0:T(8,128)(2,1)} %get-tuple-element.9) | data formatting | bytes 1572864 | tf_op jit(solution)/shard_map/reshape;squeeze | solution.py:34
  105.6 1.0 copy.19
  106.6 6.4 %gather_fusion = bf16[288,64,128]{2,1,0:T(8,128)(2,1)} fusion(bf16[2,24,64,128]{3,2,1,0:T(8,128)(2,1)S(1)} %bitcast.53, s32[288]{0:T(512)S(1)} %reshape.68), kind=kCustom, calls=%fused_computation | custom fusion | bytes 9439488 | tf_op jit(solution)/shard_map/vmap()/gather | solution.py:36
  113.0 6.3 %gather_fusion.1 = bf16[288,64,128]{2,1,0:T(8,128)(2,1)} fusion(bf16[2,24,64,128]{3,2,1,0:T(8,128)(2,1)S(1)} %bitcast.54, s32[288]{0:T(512)S(1)} %reshape.68), kind=kCustom, calls=%fused_computation.1 | custom fusion | bytes 9439488 | tf_op jit(solution)/shard_map/vmap()/gather | solution.py:37
  119.3 4.5 %fusion.26 = (f32[2,8,64]{2,1,0:T(8,128)S(1)}, bf16[2,8,64,1152]{3,2,1,0:T(8,128)(2,1)S(1)}) fusion(f32[2,8,1152]{2,1,0:T(8,128)S(1)} %mul.100, bf16[2,8,1152,128]{3,2,1,0:T(8,128)(2,1)} %bitcast.56, bf16[2,8,64,128]{3,0,2,1:T(2,128)(2,1)S(1)} %fusion.18), kind=kOutput, calls=%fused_computation.35 | convolution fusion | flops 306707456 | bytes 7417856 | tf_op jit(solution)/shard_map/hqtd,hqsd->hqts/dot_general | solution.py:41
  123.8 0.0 copy-done
  123.8 1.1 fusion.13
  124.9 0.3 copy.20
  125.2 0.7 copy.31
  125.9 0.0 all-gather.6.cloned.1.call-update
  126.0 0.0 all-gather.8.cloned.1.call-done
  126.0 62.4 %all-gather.6.cloned.1.call-done = bf16[512,4096]{1,0:T(8,128)(2,1)} async-done(((bf16[512,256]{1,0:T(8,128)(2,1)}), bf16[512,4096]{1,0:T(8,128)(2,1)}) %all-gather.6.cloned.1.call-update) | async-done | bytes 4194320 | tf_op jit(solution)/shard_map/all_gather | solution.py:87
  188.4 6.3 %convolution_convert_fusion = bf16[512,384]{1,0:T(8,128)(2,1)} fusion(bf16[512,4096]{1,0:T(8,128)(2,1)} %all-gather.6.cloned.1.call-done, bf16[384,4096]{1,0:T(8,128)(2,1)} %all-gather.8.cloned.1.call-done), kind=kOutput, calls=%fused_computation.10 | convolution fusion | flops 1610809344 | bytes 7733248 | tf_op jit(solution)/shard_map/dot_general | solution.py:86
  (5 shorter events, 0.1 us)
Async XLA Ops:
  6.5 67.6 %all-gather.4.cloned.1.call-start = ((), (), s32[]{:S(2)}) async-start(), calls=%async_computation | async-start | bytes 10027008 | tf_op jit(solution)/shard_map/all_gather | solution.py:72
  8.7 117.3 %all-gather.8.cloned.1.call-start = ((), (), s32[]{:S(2)}) async-start(), calls=%async_computation.2 | async-start | bytes 3342336 | tf_op jit(solution)/shard_map/all_gather | solution.py:84
  9.5 178.9 %all-gather.6.cloned.1.call-start = ((), (), s32[]{:S(2)}) async-start(), calls=%async_computation.1 | async-start | bytes 4456448 | tf_op jit(solution)/shard_map/all_gather | solution.py:87
  10.2 73.7 %copy-start.1 = (f32[256]{0:T(256)S(1)}, f32[256]{0:T(256)}, u32[]{:S(2)}) copy-start(f32[256]{0:T(256)} %param.11) | copy-start | bytes 3076
  83.7 5.8 %copy-start.3 = (s32[2,8]{1,0:T(2,128)S(1)}, s32[2,8]{1,0:T(2,128)}, u32[]{:S(2)}) copy-start(s32[2,8]{1,0:T(2,128)} %param.13) | copy-start | bytes 196
  83.8 6.8 %copy-start.2 = (f32[256]{0:T(256)S(1)}, f32[256]{0:T(256)}, u32[]{:S(2)}) copy-start(f32[256]{0:T(256)} %param.10) | copy-start | bytes 3076
  84.2 10.4 %collective-permute-start = (bf16[2,512,256]{1,2,0:T(8,128)(2,1)S(1)}, bf16[2,512,256]{1,2,0:T(8,128)(2,1)}, u32[]{:S(2)}, u32[]{:S(2)}) collective-permute-start(bf16[2,512,256]{1,2,0:T(8,128)(2,1)S(1)} %pad_maximum_fusion.1), channel_id=1, source_target_pairs={{0,1},{1,2},{2,3},{3,4},{4,5},{5,6},{6,7},{7,8},{8,9},{9,10},{10,1... | collective-permute-start | bytes 1572872 | tf_op jit(solution)/shard_map/ppermute | solution.py:15
  86.1 12.9 %collective-permute-start.1 = (bf16[2,512,256]{1,2,0:T(8,128)(2,1)S(1)}, bf16[2,512,256]{1,2,0:T(8,128)(2,1)}, u32[]{:S(2)}, u32[]{:S(2)}) collective-permute-start(bf16[2,512,256]{1,2,0:T(8,128)(2,1)S(1)} %pad_maximum_fusion.1), channel_id=1, source_target_pairs={{1,0},{2,1},{3,2},{4,3},{5,4},{6,5},{7,6},{8,7},{9,8},{10,9},{11,1... | collective-permute-start | bytes 1572872 | tf_op jit(solution)/shard_map/ppermute | solution.py:18
  119.3 4.5 %copy-start = (bf16[288,64,128]{2,1,0:T(8,128)(2,1)S(1)}, bf16[288,64,128]{2,1,0:T(8,128)(2,1)}, u32[]{:S(2)}) copy-start(bf16[288,64,128]{2,1,0:T(8,128)(2,1)} %gather_fusion.1) | copy-start | bytes 14155780
Sparse Core Ops, SparseCore 0:
  9.1 64.9 all-gather.3
  75.9 45.6 all-gather.7
  126.1 62.2 all-gather.5
where the time goes:
time: 202 us; the launch traced here: 201 us
  waiting for transfers between devices  135 us (67%)
  local copies, waits for them, and re-layouts  23 us (11%)
  matrix products  21.4 us (11%)
  between operations  13.3 us (7%)
  starting transfers between devices  5.36 us (3%)
  other arithmetic  3.22 us (2%)
    all_gather x1, waiting for transfers between devices, body(): lax.all_gather(proj_weight, 'ctx', axis=1, tiled=True)  64 us
    all_gather x1, waiting for transfers between devices, body(): lax.all_gather(attended, 'dp', axis=1, tiled=True)  62.4 us
    gather x3, local copies, waits for them, and re-layouts, attend(): lookup[indices]  12.7 us
    dot_general x1, matrix products, body(): jnp.einsum('tn,cnw->ctw', columns, lax.all_gather(proj_weight, 'ctx', axi...  9.52 us
    dot_general x1, matrix products, body(): lax.dot_general(lax.all_gather(attended, 'dp', axis=1, tiled=True), colum...  6.26 us
    dot_general x1, matrix products, attend(): jnp.einsum('hqtd,hqsd->hqts', query_tiles, picked_keys, preferred_element...  4.49 us
    ppermute x1, waiting for transfers between devices, padded(): lax.ppermute(lax.slice_in_dim(block, 0, width, axis=dim), axis, backward)  4.43 us
  transfers between devices with their start and end apart: 5, of which 4 were waited for; matrix products, arithmetic and copies ran while one was open for 19% of the time, Pallas kernels for 0%

commit v1 on v0

--- a/solution.py
+++ b/solution.py
@@ -5,6 +5,22 @@
 
 TILE = 64
 eps = 1e-06
+
+
+def ring_product(value, axis, dim, product):
+    size, place, rows = (lax.axis_size(axis), lax.axis_index(axis), value.shape[dim])
+    right = [(i, (i + 1) % size) for i in range(size)]
+    left = [(i, (i - 1) % size) for i in range(size)]
+    half = size // 2
+    from_left = from_right = value
+    so_far = product(value, place * rows)
+    for step in range(1, half + 1):
+        from_left = lax.ppermute(from_left, axis, right)
+        if step < size - half:
+            from_right = lax.ppermute(from_right, axis, left)
+            so_far = so_far + product(from_right, (place + step) % size * rows)
+        so_far = so_far + product(from_left, (place - step) % size * rows)
+    return so_far
 
 
 def padded(block, sides, width):
@@ -66,11 +82,16 @@
     layer_tiles = key_tiles.shape[1]
     tok_count = frames.shape[0]
     columns = frames
-    proj = jnp.einsum(
-        "tn,cnw->ctw",
-        columns,
-        lax.all_gather(proj_weight, "ctx", axis=1, tiled=True),
-        preferred_element_type=jnp.float32,
+    proj = ring_product(
+        proj_weight,
+        "ctx",
+        1,
+        lambda shard, start: jnp.einsum(
+            "tn,cnw->ctw",
+            lax.dynamic_slice_in_dim(columns, start, shard.shape[1], axis=1),
+            shard,
+            preferred_element_type=jnp.float32,
+        ),
     )
     query_rows = normed(proj[0].reshape(-1, heads, head_dim), query_gain.reshape(heads, head_dim))
     key_rows = normed(proj[1].reshape(-1, heads, head_dim), key_gain.reshape(heads, head_dim))

time: 202 us -> 228 us (1.13)
  starting transfers between devices: 5.36 us -> 62.4 us
  waiting for transfers between devices: 135 us -> 92.1 us
  matrix products: 21.4 us -> 32.8 us
    all_gather x1 -> x0, waiting for transfers between devices: 64 us -> none  [body(): lax.all_gather(proj_weight, 'ctx', axis=1, tiled=True)]
    ppermute x0 -> x15, starting transfers between devices: none -> 49.2 us  [the longest x7 33.3 us: ring_product(): from_right = lax.ppermute(from_right, axis, left)]
    ppermute x0 -> x15, waiting for transfers between devices: none -> 22.4 us  [the longest x8 21 us: ring_product(): from_left = lax.ppermute(from_left, axis, right)]
    dot_general x1 -> x16, matrix products: 9.52 us -> 21 us  [body(): jnp.einsum('tn,cnw->ctw', lax.dynamic_slice_in_dim(columns, start, shard....]
    ppermute x1, starting transfers between devices: 3.35 us -> 11 us  [padded(): lax.ppermute(lax.slice_in_dim(block, 0, width, axis=dim), axis, backward)]
    all_gather x1, waiting for transfers between devices: 62.4 us -> 69.7 us  [body(): lax.all_gather(attended, 'dp', axis=1, tiled=True)]
    ppermute x1, waiting for transfers between devices: 4.43 us -> 0.01 us  [padded(): lax.ppermute(lax.slice_in_dim(block, 0, width, axis=dim), axis, backward)]
    ppermute x1, waiting for transfers between devices: 3.31 us -> 0.01 us  [padded(): lax.ppermute(lax.slice_in_dim(block, block.shape[dim] - width, None, axis...]
  transfers between devices with their start and end apart: 5 -> 19, of which waited for: 4 -> 9; matrix products, arithmetic and copies ran while one was open for 19% -> 22% of each run, Pallas kernels for 0% -> 0%
where the time goes in v1:
time: 228 us; the launch traced here: 227 us
  waiting for transfers between devices  92.1 us (40%)
  starting transfers between devices  62.4 us (27%)
  matrix products  32.8 us (14%)
  local copies, waits for them, and re-layouts  22.2 us (10%)
  between operations  14.1 us (6%)
  other arithmetic  3.32 us (1%)
    all_gather x1, waiting for transfers between devices, body(): lax.all_gather(attended, 'dp', axis=1, tiled=True)  69.7 us
    ppermute x7, starting transfers between devices, ring_product(): from_right = lax.ppermute(from_right, axis, left)  33.3 us
    ppermute x8, waiting for transfers between devices, ring_product(): from_left = lax.ppermute(from_left, axis, right)  21 us
    dot_general x16, matrix products, body(): jnp.einsum('tn,cnw->ctw', lax.dynamic_slice_in_dim(columns, start, shard....  21 us
    ppermute x8, starting transfers between devices, ring_product(): from_left = lax.ppermute(from_left, axis, right)  16 us
    gather x3, local copies, waits for them, and re-layouts, attend(): lookup[indices]  12.6 us
    ppermute x1, starting transfers between devices, padded(): lax.ppermute(lax.slice_in_dim(block, 0, width, axis=dim), axis, backward)  11 us
    dot_general x1, matrix products, body(): lax.dot_general(lax.all_gather(attended, 'dp', axis=1, tiled=True), colum...  6.26 us
  transfers between devices with their start and end apart: 19, of which 9 were waited for; matrix products, arithmetic and copies ran while one was open for 22% of the time, Pallas kernels for 0%

profile of v1, /device:TPU:1, one launch (start us, length us, event | category | flops | bytes accessed | tf_op | source)
XLA Modules:
  0.0 227.0 jit_solution(13532312115436716568)
XLA Ops:
  6.5 1.4 copy.15
  7.9 3.0 %collective-permute-start.1 = (bf16[3,384,256]{1,2,0:T(8,128)(2,1)S(1)}, bf16[3,384,256]{1,2,0:T(8,128)(2,1)S(1)}, u32[]{:S(2)}, u32[]{:S(2)}) collective-permute-start(bf16[3,384,256]{1,2,0:T(8,128)(2,1)S(1)} %copy.15), channel_id=1, source_target_pairs={{0,1},{1,2},{2,3},{3,4},{4,5},{5,6},{6,7},{7,8},{8,9},{9,10},{10,1... | collective-permute-start | bytes 1769480 | tf_op jit(solution)/shard_map/ppermute | solution.py:18
  11.2 6.6 %collective-permute-done.1 = bf16[3,384,256]{1,2,0:T(8,128)(2,1)S(1)} collective-permute-done((bf16[3,384,256]{1,2,0:T(8,128)(2,1)S(1)}, bf16[3,384,256]{1,2,0:T(8,128)(2,1)S(1)}, u32[]{:S(2)}, u32[]{:S(2)}) %collective-permute-start.1) | collective-permute-done | bytes 589856 | tf_op jit(solution)/shard_map/ppermute | solution.py:18
  17.8 2.5 %collective-permute-start.3 = (bf16[3,384,256]{1,2,0:T(8,128)(2,1)S(1)}, bf16[3,384,256]{1,2,0:T(8,128)(2,1)S(1)}, u32[]{:S(2)}, u32[]{:S(2)}) collective-permute-start(bf16[3,384,256]{1,2,0:T(8,128)(2,1)S(1)} %collective-permute-done.1), channel_id=1, source_target_pairs={{0,1},{1,2},{2,3},{3,4},{4,5},{5,6},{6,7},{7,8},{8,9},{9,10},{10,1... | collective-permute-start | bytes 1769480 | tf_op jit(solution)/shard_map/ppermute | solution.py:18
  20.6 1.8 collective-permute-start.2
  22.3 4.8 %collective-permute-done.3 = bf16[3,384,256]{1,2,0:T(8,128)(2,1)S(1)} collective-permute-done((bf16[3,384,256]{1,2,0:T(8,128)(2,1)S(1)}, bf16[3,384,256]{1,2,0:T(8,128)(2,1)S(1)}, u32[]{:S(2)}, u32[]{:S(2)}) %collective-permute-start.3) | collective-permute-done | bytes 589856 | tf_op jit(solution)/shard_map/ppermute | solution.py:18
  27.1 2.5 %collective-permute-start.5 = (bf16[3,384,256]{1,2,0:T(8,128)(2,1)S(1)}, bf16[3,384,256]{1,2,0:T(8,128)(2,1)}, u32[]{:S(2)}, u32[]{:S(2)}) collective-permute-start(bf16[3,384,256]{1,2,0:T(8,128)(2,1)S(1)} %collective-permute-done.3), channel_id=1, source_target_pairs={{0,1},{1,2},{2,3},{3,4},{4,5},{5,6},{6,7},{7,8},{8,9},{9,10},{10,1... | collective-permute-start | bytes 1769480 | tf_op jit(solution)/shard_map/ppermute | solution.py:18
  30.2 2.8 %collective-permute-start.4 = (bf16[3,384,256]{1,2,0:T(8,128)(2,1)}, bf16[3,384,256]{1,2,0:T(8,128)(2,1)}, u32[]{:S(2)}, u32[]{:S(2)}) collective-permute-start(bf16[3,384,256]{1,2,0:T(8,128)(2,1)} %collective-permute-done.2), channel_id=1, source_target_pairs={{0,15},{1,0},{2,1},{3,2},{4,3},{5,4},{6,5},{7,6},{8,7},{9,8},{10,9... | collective-permute-start | bytes 1769480 | tf_op jit(solution)/shard_map/ppermute | solution.py:20
  32.9 1.8 fusion.42
  34.8 1.7 collective-permute-done.5
  36.4 2.6 %collective-permute-start.7 = (bf16[3,384,256]{1,2,0:T(8,128)(2,1)}, bf16[3,384,256]{1,2,0:T(8,128)(2,1)}, u32[]{:S(2)}, u32[]{:S(2)}) collective-permute-start(bf16[3,384,256]{1,2,0:T(8,128)(2,1)} %collective-permute-done.5), channel_id=1, source_target_pairs={{0,1},{1,2},{2,3},{3,4},{4,5},{5,6},{6,7},{7,8},{8,9},{9,10},{10,1... | collective-permute-start | bytes 1769480 | tf_op jit(solution)/shard_map/ppermute | solution.py:18
  39.3 1.9 fusion.38
  41.3 4.5 %collective-permute-start.6 = (bf16[3,384,256]{1,2,0:T(8,128)(2,1)}, bf16[3,384,256]{1,2,0:T(8,128)(2,1)S(1)}, u32[]{:S(2)}, u32[]{:S(2)}) collective-permute-start(bf16[3,384,256]{1,2,0:T(8,128)(2,1)} %collective-permute-done.4), channel_id=1, source_target_pairs={{0,15},{1,0},{2,1},{3,2},{4,3},{5,4},{6,5},{7,6},{8,7},{9,8},{10,9... | collective-permute-start | bytes 1769480 | tf_op jit(solution)/shard_map/ppermute | solution.py:20
  45.7 1.8 fusion.40
  47.5 0.7 collective-permute-done.7
  48.3 2.5 %collective-permute-start.9 = (bf16[3,384,256]{1,2,0:T(8,128)(2,1)}, bf16[3,384,256]{1,2,0:T(8,128)(2,1)S(1)}, u32[]{:S(2)}, u32[]{:S(2)}) collective-permute-start(bf16[3,384,256]{1,2,0:T(8,128)(2,1)} %collective-permute-done.7), channel_id=1, source_target_pairs={{0,1},{1,2},{2,3},{3,4},{4,5},{5,6},{6,7},{7,8},{8,9},{9,10},{10,1... | collective-permute-start | bytes 1769480 | tf_op jit(solution)/shard_map/ppermute | solution.py:18
  50.7 1.8 fusion.34
  52.5 1.7 fusion.36
  54.2 7.8 %collective-permute-start.8 = (bf16[3,384,256]{1,2,0:T(8,128)(2,1)S(1)}, bf16[3,384,256]{1,2,0:T(8,128)(2,1)S(1)}, u32[]{:S(2)}, u32[]{:S(2)}) collective-permute-start(bf16[3,384,256]{1,2,0:T(8,128)(2,1)S(1)} %collective-permute-done.6), channel_id=1, source_target_pairs={{0,15},{1,0},{2,1},{3,2},{4,3},{5,4},{6,5},{7,6},{8,7},{9,8},{10,9... | collective-permute-start | bytes 1769480 | tf_op jit(solution)/shard_map/ppermute | solution.py:20
  62.1 1.7 fusion.30
  63.8 1.2 collective-permute-start.11
  65.0 1.7 fusion.32
  66.6 1.7 fusion.26
  68.4 8.5 %collective-permute-start.10 = (bf16[3,384,256]{1,2,0:T(8,128)(2,1)S(1)}, bf16[3,384,256]{1,2,0:T(8,128)(2,1)S(1)}, u32[]{:S(2)}, u32[]{:S(2)}) collective-permute-start(bf16[3,384,256]{1,2,0:T(8,128)(2,1)S(1)} %collective-permute-done.8), channel_id=1, source_target_pairs={{0,15},{1,0},{2,1},{3,2},{4,3},{5,4},{6,5},{7,6},{8,7},{9,8},{10,9... | collective-permute-start | bytes 1769480 | tf_op jit(solution)/shard_map/ppermute | solution.py:20
  77.5 1.4 collective-permute-start.13
  79.5 0.6 fusion.24
  80.7 7.7 %collective-permute-start.12 = (bf16[3,384,256]{1,2,0:T(8,128)(2,1)S(1)}, bf16[3,384,256]{1,2,0:T(8,128)(2,1)S(1)}, u32[]{:S(2)}, u32[]{:S(2)}) collective-permute-start(bf16[3,384,256]{1,2,0:T(8,128)(2,1)S(1)} %collective-permute-done.10), channel_id=1, source_target_pairs={{0,15},{1,0},{2,1},{3,2},{4,3},{5,4},{6,5},{7,6},{8,7},{9,8},{10,9... | collective-permute-start | bytes 1769480 | tf_op jit(solution)/shard_map/ppermute | solution.py:20
  89.9 0.6 fusion.14
  90.5 0.6 fusion.16
  91.1 7.3 %collective-permute-done.14 = bf16[3,384,256]{1,2,0:T(8,128)(2,1)} collective-permute-done((bf16[3,384,256]{1,2,0:T(8,128)(2,1)S(1)}, bf16[3,384,256]{1,2,0:T(8,128)(2,1)}, u32[]{:S(2)}, u32[]{:S(2)}) %collective-permute-start.14) | collective-permute-done | bytes 589856 | tf_op jit(solution)/shard_map/ppermute | solution.py:18
  98.4 2.7 %add_bitcast_fusion = f32[3,512,256]{1,2,0:T(8,128)S(1)} fusion(f32[512,3,256]{0,2,1:T(8,128)S(1)} %fusion.14, f32[512,3,256]{0,2,1:T(8,128)S(1)} %fusion.16, f32[512,3,256]{0,2,1:T(8,128)S(1)} %fusion.18, f32[512,3,256]{0,2,1:T(8,128)S(1)} %fusion.20, f32[512,3,256]{0,2,1:T(8,128)S(1)} %fusion.22, f32[512,3,256]{0,2,1:T(8,128)S(1)} %fusion.24, ...), kind=kOutput, calls=%fused_computation.7 | convolution fusion | flops 307888128 | bytes 26148868 | tf_op jit(solution)/shard_map/tn,cnw->ctw/dot_general | solution.py:89
  101.5 0.8 pad_maximum_fusion.1
  102.3 2.2 collective-permute-start.15
  104.5 11.0 %collective-permute-start.16 = (bf16[2,512,256]{1,2,0:T(8,128)(2,1)}, bf16[2,512,256]{1,2,0:T(8,128)(2,1)}, u32[]{:S(2)}, u32[]{:S(2)}) collective-permute-start(bf16[2,512,256]{1,2,0:T(8,128)(2,1)} %pad_maximum_fusion.1), channel_id=1, source_target_pairs={{1,0},{2,1},{3,2},{4,3},{5,4},{6,5},{7,6},{8,7},{9,8},{10,9},{11,1... | collective-permute-start | bytes 1572872 | tf_op jit(solution)/shard_map/ppermute | solution.py:34
  116.6 0.7 fusion.60
  117.4 1.3 pad_maximum_fusion
  118.7 1.0 fusion.83
  119.7 0.9 reshape.103
  120.6 1.0 copy.20
  121.6 2.4 %reshape.104 = bf16[24,64,2,128]{1,0,3,2:T(8,128)(2,1)S(1)} reshape(bf16[1,1536,256]{1,2,0:T(8,128)(2,1)} %get-tuple-element.9) | data formatting | bytes 1572864 | tf_op jit(solution)/shard_map/reshape;squeeze | solution.py:50
  124.0 1.0 copy.23
  125.0 6.3 %gather_fusion = bf16[288,64,128]{2,1,0:T(8,128)(2,1)} fusion(bf16[2,24,64,128]{3,2,1,0:T(8,128)(2,1)S(1)} %bitcast.111, s32[288]{0:T(512)S(1)} %reshape.68), kind=kCustom, calls=%fused_computation | custom fusion | bytes 9439488 | tf_op jit(solution)/shard_map/vmap()/gather | solution.py:52
  131.3 6.2 %gather_fusion.1 = bf16[288,64,128]{2,1,0:T(8,128)(2,1)} fusion(bf16[2,24,64,128]{3,2,1,0:T(8,128)(2,1)S(1)} %bitcast.112, s32[288]{0:T(512)S(1)} %reshape.68), kind=kCustom, calls=%fused_computation.1 | custom fusion | bytes 9439488 | tf_op jit(solution)/shard_map/vmap()/gather | solution.py:53
  137.5 4.5 %fusion.84 = (f32[2,8,64]{2,1,0:T(8,128)S(1)}, bf16[2,8,64,1152]{3,2,1,0:T(8,128)(2,1)S(1)}) fusion(f32[2,8,1152]{2,1,0:T(8,128)S(1)} %mul.164, bf16[2,8,1152,128]{3,2,1,0:T(8,128)(2,1)} %bitcast.114, bf16[2,8,64,128]{3,0,2,1:T(2,128)(2,1)S(1)} %fusion.60), kind=kOutput, calls=%fused_computation.96 | convolution fusion | flops 306707456 | bytes 7417856 | tf_op jit(solution)/shard_map/hqtd,hqsd->hqts/dot_general | solution.py:57
  142.0 1.1 fusion.8
  143.4 0.7 copy.36
  144.2 69.7 %all-gather.3.cloned.1.call-done = bf16[512,4096]{1,0:T(8,128)(2,1)} async-done(((bf16[512,256]{1,0:T(8,128)(2,1)}), bf16[512,4096]{1,0:T(8,128)(2,1)}) %all-gather.3.cloned.1.call-update) | async-done | bytes 4194320 | tf_op jit(solution)/shard_map/all_gather | solution.py:108
  213.9 6.3 %convolution_convert_fusion = bf16[512,384]{1,0:T(8,128)(2,1)} fusion(bf16[512,4096]{1,0:T(8,128)(2,1)} %all-gather.3.cloned.1.call-done, bf16[384,4096]{1,0:T(8,128)(2,1)} %all-gather.5.cloned.1.call-done), kind=kOutput, calls=%fused_computation.8 | convolution fusion | flops 1610809344 | bytes 7733248 | tf_op jit(solution)/shard_map/dot_general | solution.py:107
  (57 shorter events, 6.1 us)
Async XLA Ops:
  6.5 32.5 %copy-start.5 = (s32[2,8,18]{2,1,0:T(8,128)S(1)}, s32[2,8,18]{2,1,0:T(8,128)}, u32[]{:S(2)}) copy-start(s32[2,8,18]{2,1,0:T(8,128)} %param.12) | copy-start | bytes 3460
  6.5 137.7 %all-gather.5.cloned.1.call-start = ((), (), s32[]{:S(2)}) async-start(), calls=%async_computation.1 | async-start | bytes 3342336 | tf_op jit(solution)/shard_map/all_gather | solution.py:105
  7.9 9.9 %collective-permute-start.1 = (bf16[3,384,256]{1,2,0:T(8,128)(2,1)S(1)}, bf16[3,384,256]{1,2,0:T(8,128)(2,1)S(1)}, u32[]{:S(2)}, u32[]{:S(2)}) collective-permute-start(bf16[3,384,256]{1,2,0:T(8,128)(2,1)S(1)} %copy.15), channel_id=1, source_target_pairs={{0,1},{1,2},{2,3},{3,4},{4,5},{5,6},{6,7},{7,8},{8,9},{9,10},{10,1... | collective-permute-start | bytes 1769480 | tf_op jit(solution)/shard_map/ppermute | solution.py:18
  11.0 9.6 %collective-permute-start = (bf16[3,384,256]{1,2,0:T(8,128)(2,1)S(1)}, bf16[3,384,256]{1,2,0:T(8,128)(2,1)S(1)}, u32[]{:S(2)}, u32[]{:S(2)}) collective-permute-start(bf16[3,384,256]{1,2,0:T(8,128)(2,1)S(1)} %copy.15), channel_id=1, source_target_pairs={{0,15},{1,0},{2,1},{3,2},{4,3},{5,4},{6,5},{7,6},{8,7},{9,8},{10,9... | collective-permute-start | bytes 1769480 | tf_op jit(solution)/shard_map/ppermute | solution.py:20
  17.8 9.3 %copy-start.4 = (bf16[3,384,256]{1,2,0:T(8,128)(2,1)}, bf16[3,384,256]{1,2,0:T(8,128)(2,1)S(1)}, u32[]{:S(2)}) copy-start(bf16[3,384,256]{1,2,0:T(8,128)(2,1)S(1)} %collective-permute-done.1) | copy-start | bytes 1769476
  17.8 9.3 %collective-permute-start.3 = (bf16[3,384,256]{1,2,0:T(8,128)(2,1)S(1)}, bf16[3,384,256]{1,2,0:T(8,128)(2,1)S(1)}, u32[]{:S(2)}, u32[]{:S(2)}) collective-permute-start(bf16[3,384,256]{1,2,0:T(8,128)(2,1)S(1)} %collective-permute-done.1), channel_id=1, source_target_pairs={{0,1},{1,2},{2,3},{3,4},{4,5},{5,6},{6,7},{7,8},{8,9},{9,10},{10,1... | collective-permute-start | bytes 1769480 | tf_op jit(solution)/shard_map/ppermute | solution.py:18
  20.6 9.6 %copy-start.3 = (bf16[3,384,256]{1,2,0:T(8,128)(2,1)}, bf16[3,384,256]{1,2,0:T(8,128)(2,1)S(1)}, u32[]{:S(2)}) copy-start(bf16[3,384,256]{1,2,0:T(8,128)(2,1)S(1)} %collective-permute-done) | copy-start | bytes 1769476
  20.6 9.6 %collective-permute-start.2 = (bf16[3,384,256]{1,2,0:T(8,128)(2,1)S(1)}, bf16[3,384,256]{1,2,0:T(8,128)(2,1)}, u32[]{:S(2)}, u32[]{:S(2)}) collective-permute-start(bf16[3,384,256]{1,2,0:T(8,128)(2,1)S(1)} %collective-permute-done), channel_id=1, source_target_pairs={{0,15},{1,0},{2,1},{3,2},{4,3},{5,4},{6,5},{7,6},{8,7},{9,8},{10,9... | collective-permute-start | bytes 1769480 | tf_op jit(solution)/shard_map/ppermute | solution.py:20
  27.1 12.2 %copy-start.2 = (bf16[3,384,256]{1,2,0:T(8,128)(2,1)}, bf16[3,384,256]{1,2,0:T(8,128)(2,1)S(1)}, u32[]{:S(2)}) copy-start(bf16[3,384,256]{1,2,0:T(8,128)(2,1)S(1)} %collective-permute-done.3) | copy-start | bytes 1769476
  27.1 9.3 %collective-permute-start.5 = (bf16[3,384,256]{1,2,0:T(8,128)(2,1)S(1)}, bf16[3,384,256]{1,2,0:T(8,128)(2,1)}, u32[]{:S(2)}, u32[]{:S(2)}) collective-permute-start(bf16[3,384,256]{1,2,0:T(8,128)(2,1)S(1)} %collective-permute-done.3), channel_id=1, source_target_pairs={{0,1},{1,2},{2,3},{3,4},{4,5},{5,6},{6,7},{7,8},{8,9},{9,10},{10,1... | collective-permute-start | bytes 1769480 | tf_op jit(solution)/shard_map/ppermute | solution.py:18
  29.6 184.3 %all-gather.3.cloned.1.call-start = ((), (), s32[]{:S(2)}) async-start(), calls=%async_computation | async-start | bytes 4456448 | tf_op jit(solution)/shard_map/all_gather | solution.py:108
  30.2 11.1 %collective-permute-start.4 = (bf16[3,384,256]{1,2,0:T(8,128)(2,1)}, bf16[3,384,256]{1,2,0:T(8,128)(2,1)}, u32[]{:S(2)}, u32[]{:S(2)}) collective-permute-start(bf16[3,384,256]{1,2,0:T(8,128)(2,1)} %collective-permute-done.2), channel_id=1, source_target_pairs={{0,15},{1,0},{2,1},{3,2},{4,3},{5,4},{6,5},{7,6},{8,7},{9,8},{10,9... | collective-permute-start | bytes 1769480 | tf_op jit(solution)/shard_map/ppermute | solution.py:20
  36.4 11.8 %collective-permute-start.7 = (bf16[3,384,256]{1,2,0:T(8,128)(2,1)}, bf16[3,384,256]{1,2,0:T(8,128)(2,1)}, u32[]{:S(2)}, u32[]{:S(2)}) collective-permute-start(bf16[3,384,256]{1,2,0:T(8,128)(2,1)} %collective-permute-done.5), channel_id=1, source_target_pairs={{0,1},{1,2},{2,3},{3,4},{4,5},{5,6},{6,7},{7,8},{8,9},{9,10},{10,1... | collective-permute-start | bytes 1769480 | tf_op jit(solution)/shard_map/ppermute | solution.py:18
  39.3 13.2 %copy-start = (bf16[512,6144]{1,0:T(8,128)(2,1)S(1)}, bf16[512,6144]{1,0:T(8,128)(2,1)}, u32[]{:S(2)}) copy-start(bf16[512,6144]{1,0:T(8,128)(2,1)} %param.7) | copy-start | bytes 18874372
  41.3 13.0 %collective-permute-start.6 = (bf16[3,384,256]{1,2,0:T(8,128)(2,1)}, bf16[3,384,256]{1,2,0:T(8,128)(2,1)S(1)}, u32[]{:S(2)}, u32[]{:S(2)}) collective-permute-start(bf16[3,384,256]{1,2,0:T(8,128)(2,1)} %collective-permute-done.4), channel_id=1, source_target_pairs={{0,15},{1,0},{2,1},{3,2},{4,3},{5,4},{6,5},{7,6},{8,7},{9,8},{10,9... | collective-permute-start | bytes 1769480 | tf_op jit(solution)/shard_map/ppermute | solution.py:20
  48.3 15.5 %collective-permute-start.9 = (bf16[3,384,256]{1,2,0:T(8,128)(2,1)}, bf16[3,384,256]{1,2,0:T(8,128)(2,1)S(1)}, u32[]{:S(2)}, u32[]{:S(2)}) collective-permute-start(bf16[3,384,256]{1,2,0:T(8,128)(2,1)} %collective-permute-done.7), channel_id=1, source_target_pairs={{0,1},{1,2},{2,3},{3,4},{4,5},{5,6},{6,7},{7,8},{8,9},{9,10},{10,1... | collective-permute-start | bytes 1769480 | tf_op jit(solution)/shard_map/ppermute | solution.py:18
  54.2 14.1 %collective-permute-start.8 = (bf16[3,384,256]{1,2,0:T(8,128)(2,1)S(1)}, bf16[3,384,256]{1,2,0:T(8,128)(2,1)S(1)}, u32[]{:S(2)}, u32[]{:S(2)}) collective-permute-start(bf16[3,384,256]{1,2,0:T(8,128)(2,1)S(1)} %collective-permute-done.6), channel_id=1, source_target_pairs={{0,15},{1,0},{2,1},{3,2},{4,3},{5,4},{6,5},{7,6},{8,7},{9,8},{10,9... | collective-permute-start | bytes 1769480 | tf_op jit(solution)/shard_map/ppermute | solution.py:20
  63.8 13.7 %collective-permute-start.11 = (bf16[3,384,256]{1,2,0:T(8,128)(2,1)S(1)}, bf16[3,384,256]{1,2,0:T(8,128)(2,1)S(1)}, u32[]{:S(2)}, u32[]{:S(2)}) collective-permute-start(bf16[3,384,256]{1,2,0:T(8,128)(2,1)S(1)} %collective-permute-done.9), channel_id=1, source_target_pairs={{0,1},{1,2},{2,3},{3,4},{4,5},{5,6},{6,7},{7,8},{8,9},{9,10},{10,1... | collective-permute-start | bytes 1769480 | tf_op jit(solution)/shard_map/ppermute | solution.py:18
  68.4 12.3 %collective-permute-start.10 = (bf16[3,384,256]{1,2,0:T(8,128)(2,1)S(1)}, bf16[3,384,256]{1,2,0:T(8,128)(2,1)S(1)}, u32[]{:S(2)}, u32[]{:S(2)}) collective-permute-start(bf16[3,384,256]{1,2,0:T(8,128)(2,1)S(1)} %collective-permute-done.8), channel_id=1, source_target_pairs={{0,15},{1,0},{2,1},{3,2},{4,3},{5,4},{6,5},{7,6},{8,7},{9,8},{10,9... | collective-permute-start | bytes 1769480 | tf_op jit(solution)/shard_map/ppermute | solution.py:20
  77.5 11.6 %collective-permute-start.13 = (bf16[3,384,256]{1,2,0:T(8,128)(2,1)S(1)}, bf16[3,384,256]{1,2,0:T(8,128)(2,1)S(1)}, u32[]{:S(2)}, u32[]{:S(2)}) collective-permute-start(bf16[3,384,256]{1,2,0:T(8,128)(2,1)S(1)} %collective-permute-done.11), channel_id=1, source_target_pairs={{0,1},{1,2},{2,3},{3,4},{4,5},{5,6},{6,7},{7,8},{8,9},{9,10},{10,1... | collective-permute-start | bytes 1769480 | tf_op jit(solution)/shard_map/ppermute | solution.py:18
  80.7 9.8 %collective-permute-start.12 = (bf16[3,384,256]{1,2,0:T(8,128)(2,1)S(1)}, bf16[3,384,256]{1,2,0:T(8,128)(2,1)S(1)}, u32[]{:S(2)}, u32[]{:S(2)}) collective-permute-start(bf16[3,384,256]{1,2,0:T(8,128)(2,1)S(1)} %collective-permute-done.10), channel_id=1, source_target_pairs={{0,15},{1,0},{2,1},{3,2},{4,3},{5,4},{6,5},{7,6},{8,7},{9,8},{10,9... | collective-permute-start | bytes 1769480 | tf_op jit(solution)/shard_map/ppermute | solution.py:20
  89.0 9.4 %collective-permute-start.14 = (bf16[3,384,256]{1,2,0:T(8,128)(2,1)S(1)}, bf16[3,384,256]{1,2,0:T(8,128)(2,1)}, u32[]{:S(2)}, u32[]{:S(2)}) collective-permute-start(bf16[3,384,256]{1,2,0:T(8,128)(2,1)S(1)} %collective-permute-done.13), channel_id=1, source_target_pairs={{0,1},{1,2},{2,3},{3,4},{4,5},{5,6},{6,7},{7,8},{8,9},{9,10},{10,1... | collective-permute-start | bytes 1769480 | tf_op jit(solution)/shard_map/ppermute | solution.py:18
  91.1 10.1 %copy-start.6 = (f32[256]{0:T(256)S(1)}, f32[256]{0:T(256)}, u32[]{:S(2)}) copy-start(f32[256]{0:T(256)} %param.11) | copy-start | bytes 3076
  101.1 14.4 %copy-start.8 = (s32[2,8]{1,0:T(2,128)S(1)}, s32[2,8]{1,0:T(2,128)}, u32[]{:S(2)}) copy-start(s32[2,8]{1,0:T(2,128)} %param.13) | copy-start | bytes 196
  101.5 15.1 %copy-start.7 = (f32[256]{0:T(256)S(1)}, f32[256]{0:T(256)}, u32[]{:S(2)}) copy-start(f32[256]{0:T(256)} %param.10) | copy-start | bytes 3076
  102.3 15.0 %collective-permute-start.15 = (bf16[2,512,256]{1,2,0:T(8,128)(2,1)}, bf16[2,512,256]{1,2,0:T(8,128)(2,1)}, u32[]{:S(2)}, u32[]{:S(2)}) collective-permute-start(bf16[2,512,256]{1,2,0:T(8,128)(2,1)} %pad_maximum_fusion.1), channel_id=1, source_target_pairs={{0,1},{1,2},{2,3},{3,4},{4,5},{5,6},{6,7},{7,8},{8,9},{9,10},{10,1... | collective-permute-start | bytes 1572872 | tf_op jit(solution)/shard_map/ppermute | solution.py:31
  104.5 12.8 %collective-permute-start.16 = (bf16[2,512,256]{1,2,0:T(8,128)(2,1)}, bf16[2,512,256]{1,2,0:T(8,128)(2,1)}, u32[]{:S(2)}, u32[]{:S(2)}) collective-permute-start(bf16[2,512,256]{1,2,0:T(8,128)(2,1)} %pad_maximum_fusion.1), channel_id=1, source_target_pairs={{1,0},{2,1},{3,2},{4,3},{5,4},{6,5},{7,6},{8,7},{9,8},{10,9},{11,1... | collective-permute-start | bytes 1572872 | tf_op jit(solution)/shard_map/ppermute | solution.py:34
  137.5 4.5 %copy-start.1 = (bf16[288,64,128]{2,1,0:T(8,128)(2,1)S(1)}, bf16[288,64,128]{2,1,0:T(8,128)(2,1)}, u32[]{:S(2)}) copy-start(bf16[288,64,128]{2,1,0:T(8,128)(2,1)} %gather_fusion.1) | copy-start | bytes 14155780
Sparse Core Ops, SparseCore 0:
  29.7 55.8 all-gather.4
  144.3 69.5 all-gather.2
